TPU v7x, 512 devices: a whole 4x8x8 slice. The times are simulated.
512 devices in a mesh: tm: 16 (over y, core), nin: 8 (over z), nout: 4 (over x).
Axes of the slice: x: 4, y: 8, z: 8, core: 2. Of those that a mesh axis runs over, the one named last changes fastest.
Arguments:
- spikes: int32 [4096, 2048], P('tm', 'nin'), may hold values 0 or 1
- exposure: int32 [4096], P('tm'), may hold values from 1 to 8
- weights: bfloat16 [16384, 2048], P('nin', 'nout'), may hold values from -0.375 to 0.375
- direction: float32 [16384, 2048], P(('nin', 'tm'), 'nout'), may hold values from -6 to 6
- residual: float32 [16384, 2048], P(('nin', 'tm'), 'nout'), may hold values from -0.75 to 0.75
- iterate: float32 [16384, 2048], P(('nin', 'tm'), 'nout'), may hold values from -1.8 to 1.8
Outputs:
- new_iterate: float32 [16384, 2048], P(('nin', 'tm'), 'nout')
- new_residual: float32 [16384, 2048], P(('nin', 'tm'), 'nout')
- new_direction: float32 [16384, 2048], P(('nin', 'tm'), 'nout')
All inputs are finite; a program needn't handle non-finite values. No bound on the sum of `spikes` on one device may be relied on, other than what follows from the above.
Results may differ from a plain program's by a relative error of at most 0.015.
Values may be sent and summed in bfloat16 or wider, within the bound.
A program may use at most 64 MiB of HBM per device.

v0:
```python
import math
import jax
import jax.numpy as jnp
from jax import lax
from jax.sharding import PartitionSpec as P

BASES = 8
HISTORY = 128
RIDGE_WEIGHT = 0.05
NORM_EPS = 1e-06


def shifted(value, axis, steps):
    count = lax.axis_size(axis)
    initial, last = (max(0, -steps), min(count, count - steps))
    return lax.ppermute(value, axis, [(source, source + steps) for source in range(initial, last)])


def basis_table(history, bases_count):
    lag_values = jnp.arange(1, history + 1, dtype=jnp.float32)
    warped = jnp.log(lag_values + 1.0)
    log_low = math.log(2.0)
    log_high = math.log(history + 1.0)
    spacing = (log_high - log_low) / (bases_count - 1)
    centers = log_low + spacing * jnp.arange(bases_count, dtype=jnp.float32)
    phases = (warped[:, None] - centers[None, :]) * (math.pi / (2.0 * spacing))
    phases = jnp.clip(phases, -math.pi, math.pi)
    bump_values = 0.5 * (1.0 + jnp.cos(phases))
    bump_values = bump_values / jnp.sum(bump_values, axis=0, keepdims=True)
    return bump_values.astype(jnp.bfloat16)


def lag_kernel(basis_rows, span, offset):
    out_index = jnp.arange(span, dtype=jnp.int32)[:, None]
    in_index = jnp.arange(span, dtype=jnp.int32)[None, :]
    lag_index = out_index + offset - in_index
    is_valid = (lag_index >= 1) & (lag_index <= HISTORY)
    take_index = jnp.clip(lag_index - 1, 0, HISTORY - 1)
    return jnp.where(
        is_valid[None], jnp.take(basis_rows.T, take_index, axis=1), jnp.zeros((), jnp.bfloat16)
    )


def per_device(spikes, exposure, weights, direction, residual, iterate):
    block_rows = spikes.shape[0]
    neuron_cols = spikes.shape[1]
    basis_rows = basis_table(HISTORY, BASES)
    spike_low = spikes.astype(jnp.bfloat16)
    block_count = block_rows // HISTORY
    stacked = spike_low.reshape(block_count, HISTORY, neuron_cols)
    kernel_same = lag_kernel(basis_rows, HISTORY, 0)
    kernel_before = lag_kernel(basis_rows, HISTORY, HISTORY)
    current = jnp.einsum("bim,cmn->cinb", kernel_same, stacked, preferred_element_type=jnp.float32)
    tail_part = jnp.einsum(
        "bim,mn->inb", kernel_before, stacked[-1], preferred_element_type=jnp.float32
    )
    inner_part = jnp.einsum(
        "bim,cmn->cinb", kernel_before, stacked[:-1], preferred_element_type=jnp.float32
    )
    tail_terms = shifted(tail_part.astype(jnp.bfloat16), "tm", 1).astype(tail_part.dtype)
    own_terms = current + jnp.concatenate([tail_terms[None], inner_part], axis=0)
    features = own_terms.reshape(block_rows, neuron_cols * BASES).astype(jnp.bfloat16)
    direction_low = direction.astype(jnp.bfloat16)
    columns = features
    along_part = jnp.dot(
        columns,
        lax.all_gather(direction_low, "tm", axis=0, tiled=True),
        preferred_element_type=jnp.float32,
    )
    predictor_part = jnp.dot(features, weights, preferred_element_type=jnp.float32)
    tick_scale = exposure.astype(jnp.float32) / 8.0
    predictor_full, along_full = (
        lax.psum(predictor_part.astype(jnp.bfloat16), "nin").astype(jnp.float32),
        lax.psum(along_part.astype(jnp.bfloat16), "nin").astype(jnp.float32),
    )
    weighted = (tick_scale[:, None] * jnp.exp(predictor_full) * along_full).astype(jnp.bfloat16)
    columns = features
    gram = lax.psum_scatter(
        lax.dot_general(
            columns, weighted, (((0,), (0,)), ((), ())), preferred_element_type=jnp.float32
        ).astype(jnp.bfloat16),
        "tm",
        scatter_dimension=0,
        tiled=True,
    ).astype(jnp.float32)
    bin_total = block_rows * lax.axis_size("tm")
    curvature_prod = gram / bin_total + RIDGE_WEIGHT * direction
    old_norm, curvature = lax.psum(
        (jnp.sum(residual * residual, axis=0), jnp.sum(direction * curvature_prod, axis=0)),
        ("tm", "nin"),
    )
    step_size = old_norm / curvature
    new_iterate = iterate + step_size[None, :] * direction
    new_residual = residual - step_size[None, :] * curvature_prod
    new_norm = lax.psum(jnp.sum(new_residual * new_residual, axis=0), ("tm", "nin"))
    new_direction = new_residual + (new_norm / (old_norm + NORM_EPS))[None, :] * direction
    return (new_iterate, new_residual, new_direction)


def solution(mesh):
    in_specs = (
        P("tm", "nin"),
        P("tm"),
        P("nin", "nout"),
        P(("nin", "tm"), "nout"),
        P(("nin", "tm"), "nout"),
        P(("nin", "tm"), "nout"),
    )
    out_specs = (P(("nin", "tm"), "nout"), P(("nin", "tm"), "nout"), P(("nin", "tm"), "nout"))
    return jax.shard_map(
        per_device, mesh=mesh, in_specs=in_specs, out_specs=out_specs, check_vma=False
    )
```

profile of v0, /device:TPU:2, one launch (start us, length us, event | category | flops | bytes accessed | tf_op | source)
XLA Modules:
  0.0 800.1 jit_solution(18235166921538115580)
XLA Ops:
  7.2 0.0 copy-start
  7.2 0.0 all-gather.2.cloned.1.call-start
  7.2 1.8 convert_element_type.56
  9.0 0.0 all-gather.2.cloned.1.call-update
  9.0 0.0 all-reduce.4.cloned.1.call-start
  9.1 0.2 multiply_reduce_fusion.3
  9.3 0.1 divide_convert_fusion
  9.4 0.1 copy.17
  9.6 0.1 bitcast_clamp_fusion
  9.7 57.8 %gather_fusion.1 = bf16[16384,8]{1,0:T(8,128)(2,1)} fusion(bf16[8,128]{0,1:T(8,128)(2,1)S(1)} %copy.17, s32[16384]{0:T(1024)S(1)} %bitcast_clamp_fusion), kind=kCustom, calls=%fused_computation.1.clone | custom fusion | bytes 589824 | tf_op jit(solution)/shard_map/jit(_take)/gather | solution.py:40
  67.5 0.0 copy-start.5
  67.5 3.6 copy.20
  71.2 0.0 copy-done.5
  71.2 0.1 fusion.30
  71.3 1.1 fusion.1
  72.4 1.8 collective-permute-start
  74.2 57.8 %gather_fusion = bf16[16384,8]{1,0:T(8,128)(2,1)} fusion(bf16[8,128]{0,1:T(8,128)(2,1)S(1)} %copy.17, s32[16384]{0:T(1024)S(1)} %bitcast_clamp_fusion.1), kind=kCustom, calls=%fused_computation.clone | custom fusion | bytes 589824 | tf_op jit(solution)/shard_map/jit(_take)/gather | solution.py:40
  132.0 3.6 copy.18
  135.6 0.1 fusion.27
  135.7 0.3 convolution_bitcast_fusion
  136.0 0.0 collective-permute-done
  136.0 0.1 bitcast_convert_fusion
  136.1 0.4 fusion
  136.5 2.1 copy.21
  138.6 0.0 copy-done
  138.6 0.0 copy-start.2
  138.6 2.8 convolution_convert_fusion.3
  141.4 0.0 all-gather.2.cloned.1.call-done
  141.4 0.0 copy-done.2
  141.4 3.0 convolution_convert_fusion.2
  144.4 0.0 all-reduce.4.cloned.1.call-update
  144.5 0.0 reduce-scatter.2.cloned.1.call-start
  144.5 0.0 copy-done.7
  144.5 85.0 %all-reduce.4.cloned.1.call-done = (bf16[256,512]{1,0:T(8,128)(2,1)}, bf16[256,512]{1,0:T(8,128)(2,1)}) async-done(((bf16[256,512]{1,0:T(8,128)(2,1)}, bf16[256,512]{1,0:T(8,128)(2,1)}), (bf16[256,512]{1,0:T(8,128)(2,1)}, bf16[256,512]{1,0:T(8,128)(2,1)})) %all-reduce.4.cloned.1.call-update) | async-done | bytes 524304 | tf_op jit(solution)/shard_map/psum | solution.py:74
  229.5 0.0 copy-start.4
  229.5 3.2 convolution_convert_fusion
  232.8 0.0 copy-start.1
  232.8 0.0 reduce-scatter.2.cloned.1.call-update
  232.8 0.0 copy-done.4
  232.9 59.8 %reduce-scatter.2.cloned.1.call-done = bf16[128,512]{1,0:T(8,128)(2,1)} async-done(((bf16[2048,512]{1,0:T(8,128)(2,1)}), bf16[128,512]{1,0:T(8,128)(2,1)}) %reduce-scatter.2.cloned.1.call-update) | async-done | bytes 131088 | tf_op jit(solution)/shard_map/reduce_scatter | solution.py:78
  292.7 0.0 copy-done.1
  292.7 1.0 multiply_reduce_fusion.1
  293.6 250.6 %all-reduce = (f32[512]{0:T(512)S(1)}, f32[512]{0:T(512)S(1)}) all-reduce(f32[512]{0:T(512)S(1)} %multiply_reduce_fusion.2, f32[512]{0:T(512)S(1)} %multiply_reduce_fusion.1), channel_id=1, replica_groups=mesh['tm'=16,'nin'=8,'nout'=4] {'tm','nin'}, use_global_device_ids=true, to_apply=%region_1.2 | all-reduce | flops 1024 | bytes 8192 | tf_op jit(solution)/shard_map/psum | solution.py:88
  544.3 0.0 copy-done.6
  544.3 1.7 multiply_reduce_fusion
  546.0 246.8 %psum.39 = f32[512]{0:T(512)S(1)} all-reduce(f32[512]{0:T(512)S(1)} %get-tuple-element.8), channel_id=1, replica_groups=mesh['tm'=16,'nin'=8,'nout'=4] {'tm','nin'}, use_global_device_ids=true, to_apply=%region_9.11 | all-reduce | flops 512 | bytes 4096 | tf_op jit(solution)/shard_map/psum | solution.py:95
  792.8 0.8 multiply_add_fusion
  793.5 0.0 copy-done.3
  (12 shorter events, 0.1 us)
Async XLA Ops:
  7.2 131.5 %copy-start = (bf16[2048,512]{1,0:T(8,128)(2,1)S(1)}, bf16[2048,512]{1,0:T(8,128)(2,1)}, u32[]{:S(2)}) copy-start(bf16[2048,512]{1,0:T(8,128)(2,1)} %param.10) | copy-start | bytes 6291460
  7.2 134.2 %all-gather.2.cloned.1.call-start = ((), (), s32[]{:S(2)}) async-start(), calls=%async_computation.1 | async-start | bytes 2228224 | tf_op jit(solution)/shard_map/all_gather | solution.py:67
  9.0 220.5 %all-reduce.4.cloned.1.call-start = ((), (), s32[]{:S(2)}) async-start(), calls=%async_computation.3 | async-start | bytes 1048576 | tf_op jit(solution)/shard_map/psum | solution.py:74
  67.5 3.6 copy-start.5
  72.4 63.6 %collective-permute-start = (bf16[128,256,8]{1,0,2:T(8,128)(2,1)}, bf16[128,256,8]{1,0,2:T(8,128)(2,1)S(1)}, u32[]{:S(2)}, u32[]{:S(2)}) collective-permute-start(bf16[128,256,8]{1,0,2:T(8,128)(2,1)} %fusion.1), channel_id=1, source_target_pairs={{0,32},{32,64},{64,96},{96,128},{128,160},{160,192},{192,224},{224... | collective-permute-start | bytes 1572872 | tf_op jit(solution)/shard_map/ppermute | solution.py:16
  138.6 2.8 copy-start.2
  141.4 3.1 copy-start.7
  144.5 148.2 %reduce-scatter.2.cloned.1.call-start = ((), (), s32[]{:S(2)}) async-start(), calls=%async_computation.2 | async-start | bytes 2228224 | tf_op jit(solution)/shard_map/reduce_scatter | solution.py:78
  229.5 3.3 copy-start.4
  232.8 59.9 %copy-start.1 = (f32[128,512]{1,0:T(8,128)S(1)}, f32[128,512]{1,0:T(8,128)}, u32[]{:S(2)}) copy-start(f32[128,512]{1,0:T(8,128)} %param.11) | copy-start | bytes 786436
  232.8 311.5 %copy-start.6 = (f32[128,512]{1,0:T(8,128)S(1)}, f32[128,512]{1,0:T(8,128)}, u32[]{:S(2)}) copy-start(f32[128,512]{1,0:T(8,128)} %param.13) | copy-start | bytes 786436
  546.0 247.6 %copy-start.3 = (f32[128,512]{1,0:T(8,128)}, f32[128,512]{1,0:T(8,128)S(1)}, u32[]{:S(2)}) copy-start(f32[128,512]{1,0:T(8,128)S(1)} %get-tuple-element.9) | copy-start | bytes 786436
Sparse Core Ops, SparseCore 0:
  10.7 46.5 all-gather.1
  144.6 84.9 all-reduce.3
  232.9 59.6 reduce-scatter.1
where the time goes:
time: 800 us
  blocking collectives  497 us (62%)
  waiting for transfers between devices  145 us (18%)
  local copies, waits for them, and re-layouts  125 us (16%)
  between operations  13.9 us (2%)
  matrix products  10.8 us (1%)
    psum x1, blocking collectives, per_device(): lax.psum((jnp.sum(residual * residual, axis=0), jnp.sum(direction * curva...  251 us
    psum x1, blocking collectives, per_device(): lax.psum(jnp.sum(new_residual * new_residual, axis=0), ('tm', 'nin'))  247 us
    gather x4, local copies, waits for them, and re-layouts, lag_kernel(): jnp.take(basis_rows.T, take_index, axis=1)  123 us
    psum x1, waiting for transfers between devices, per_device(): lax.psum(along_part.astype(jnp.bfloat16), 'nin').astype(jnp.float32)  85 us
    reduce_scatter x1, waiting for transfers between devices, per_device(): lax.psum_scatter(lax.dot_general(columns, weighted, (((0,), (0,)), ((), (...  59.8 us
  transfers between devices with their start and end apart: 4, of which 2 were waited for; matrix products, arithmetic and copies ran while one was open for 16% of the time, Pallas kernels for 0%

commit v1 on v0

--- a/solution.py
+++ b/solution.py
@@ -92,7 +92,7 @@
     step_size = old_norm / curvature
     new_iterate = iterate + step_size[None, :] * direction
     new_residual = residual - step_size[None, :] * curvature_prod
-    new_norm = lax.psum(jnp.sum(new_residual * new_residual, axis=0), ("tm", "nin"))
+    new_norm = lax.psum(lax.psum(jnp.sum(new_residual * new_residual, axis=0), "tm"), "nin")
     new_direction = new_residual + (new_norm / (old_norm + NORM_EPS))[None, :] * direction
     return (new_iterate, new_residual, new_direction)
 

time: 800 us -> 591 us (0.74)
  the two profiles are of different devices: /device:TPU:2 before, /device:TPU:6 now
where the time goes in v1:
time: 591 us; the launch traced here: 590 us
  blocking collectives  288 us (49%)
  waiting for transfers between devices  145 us (25%)
  local copies, waits for them, and re-layouts  124 us (21%)
  between operations  13.9 us (2%)
  matrix products  10.8 us (2%)
  other arithmetic  6.02 us (1%)
    psum x1, blocking collectives, per_device(): lax.psum((jnp.sum(residual * residual, axis=0), jnp.sum(direction * curva...  251 us
    gather x4, local copies, waits for them, and re-layouts, lag_kernel(): jnp.take(basis_rows.T, take_index, axis=1)  122 us
    psum x1, waiting for transfers between devices, per_device(): lax.psum(along_part.astype(jnp.bfloat16), 'nin').astype(jnp.float32)  85 us
    reduce_scatter x1, waiting for transfers between devices, per_device(): lax.psum_scatter(lax.dot_general(columns, weighted, (((0,), (0,)), ((), (...  59.8 us
    psum x1, blocking collectives, per_device(): lax.psum(jnp.sum(new_residual * new_residual, axis=0), 'tm')  23.5 us
    psum x1, blocking collectives, per_device(): lax.psum(lax.psum(jnp.sum(new_residual * new_residual, axis=0), 'tm'), 'n...  14.2 us
  transfers between devices with their start and end apart: 4, of which 2 were waited for; matrix products, arithmetic and copies ran while one was open for 22% of the time, Pallas kernels for 0%

profile of v1, /device:TPU:6, one launch (start us, length us, event | category | flops | bytes accessed | tf_op | source)
XLA Modules:
  0.0 590.1 jit_solution(488128586828846715)
XLA Ops:
  7.2 0.0 copy-start
  7.2 0.0 all-gather.2.cloned.1.call-start
  7.2 1.8 convert_element_type.56
  9.0 0.0 all-gather.2.cloned.1.call-update
  9.0 0.0 all-reduce.4.cloned.1.call-start
  9.1 0.2 multiply_reduce_fusion.3
  9.3 0.1 divide_convert_fusion
  9.4 0.1 copy.17
  9.6 0.1 bitcast_clamp_fusion
  9.7 57.4 %gather_fusion.1 = bf16[16384,8]{1,0:T(8,128)(2,1)} fusion(bf16[8,128]{0,1:T(8,128)(2,1)S(1)} %copy.17, s32[16384]{0:T(1024)S(1)} %bitcast_clamp_fusion), kind=kCustom, calls=%fused_computation.1.clone | custom fusion | bytes 589824 | tf_op jit(solution)/shard_map/jit(_take)/gather | solution.py:40
  67.1 0.0 copy-start.5
  67.1 3.6 copy.20
  70.7 0.0 copy-done.5
  70.8 0.1 fusion.30
  70.9 1.1 fusion.1
  72.0 1.8 collective-permute-start
  73.8 57.4 %gather_fusion = bf16[16384,8]{1,0:T(8,128)(2,1)} fusion(bf16[8,128]{0,1:T(8,128)(2,1)S(1)} %copy.17, s32[16384]{0:T(1024)S(1)} %bitcast_clamp_fusion.1), kind=kCustom, calls=%fused_computation.clone | custom fusion | bytes 589824 | tf_op jit(solution)/shard_map/jit(_take)/gather | solution.py:40
  131.2 3.6 copy.18
  134.7 0.1 fusion.27
  134.8 0.3 convolution_bitcast_fusion
  135.1 0.0 collective-permute-done
  135.1 0.1 bitcast_convert_fusion
  135.2 0.4 fusion
  135.6 2.1 copy.21
  137.7 0.0 copy-done
  137.7 0.0 copy-start.2
  137.7 2.8 convolution_convert_fusion.3
  140.5 0.0 copy-start.7
  140.5 0.0 all-gather.2.cloned.1.call-done
  140.5 0.0 copy-done.2
  140.5 3.1 convolution_convert_fusion.2
  143.6 0.0 all-reduce.4.cloned.1.call-update
  143.6 0.0 reduce-scatter.2.cloned.1.call-start
  143.6 0.0 copy-done.7
  143.7 85.0 %all-reduce.4.cloned.1.call-done = (bf16[256,512]{1,0:T(8,128)(2,1)}, bf16[256,512]{1,0:T(8,128)(2,1)}) async-done(((bf16[256,512]{1,0:T(8,128)(2,1)}, bf16[256,512]{1,0:T(8,128)(2,1)}), (bf16[256,512]{1,0:T(8,128)(2,1)}, bf16[256,512]{1,0:T(8,128)(2,1)})) %all-reduce.4.cloned.1.call-update) | async-done | bytes 524304 | tf_op jit(solution)/shard_map/psum | solution.py:74
  228.6 3.2 convolution_convert_fusion
  231.9 0.0 reduce-scatter.2.cloned.1.call-update
  231.9 0.0 copy-done.4
  231.9 59.8 %reduce-scatter.2.cloned.1.call-done = bf16[128,512]{1,0:T(8,128)(2,1)} async-done(((bf16[2048,512]{1,0:T(8,128)(2,1)}), bf16[128,512]{1,0:T(8,128)(2,1)}) %reduce-scatter.2.cloned.1.call-update) | async-done | bytes 131088 | tf_op jit(solution)/shard_map/reduce_scatter | solution.py:78
  291.7 0.0 copy-done.1
  291.7 1.0 multiply_reduce_fusion.1
  292.7 250.7 %all-reduce = (f32[512]{0:T(512)S(1)}, f32[512]{0:T(512)S(1)}) all-reduce(f32[512]{0:T(512)S(1)} %multiply_reduce_fusion.2, f32[512]{0:T(512)S(1)} %multiply_reduce_fusion.1), channel_id=1, replica_groups=mesh['tm'=16,'nin'=8,'nout'=4] {'tm','nin'}, use_global_device_ids=true, to_apply=%region_1.2 | all-reduce | flops 1024 | bytes 8192 | tf_op jit(solution)/shard_map/psum | solution.py:88
  543.4 0.0 copy-done.6
  543.4 1.7 multiply_reduce_fusion
  545.1 23.5 %psum.46 = f32[512]{0:T(512)S(1)} all-reduce(f32[512]{0:T(512)S(1)} %get-tuple-element.8), channel_id=1, replica_groups=mesh['tm'=16,'nin'=8,'nout'=4] {'tm'}, use_global_device_ids=true, to_apply=%region_9.11 | all-reduce | flops 512 | bytes 4096 | tf_op jit(solution)/shard_map/psum | solution.py:95
  568.6 14.2 %psum.47 = f32[512]{0:T(512)S(1)} all-reduce(f32[512]{0:T(512)S(1)} %psum.46), channel_id=1, replica_groups=mesh['tm'=16,'nin'=8,'nout'=4] {'nin'}, use_global_device_ids=true, to_apply=%region_10.12 | all-reduce | flops 512 | bytes 4096 | tf_op jit(solution)/shard_map/psum | solution.py:95
  582.8 0.8 multiply_add_fusion
  583.5 0.0 copy-done.3
  (13 shorter events, 0.1 us)
Async XLA Ops:
  7.2 130.6 %copy-start = (bf16[2048,512]{1,0:T(8,128)(2,1)S(1)}, bf16[2048,512]{1,0:T(8,128)(2,1)}, u32[]{:S(2)}) copy-start(bf16[2048,512]{1,0:T(8,128)(2,1)} %param.10) | copy-start | bytes 6291460
  7.2 133.3 %all-gather.2.cloned.1.call-start = ((), (), s32[]{:S(2)}) async-start(), calls=%async_computation.1 | async-start | bytes 2228224 | tf_op jit(solution)/shard_map/all_gather | solution.py:67
  9.0 219.6 %all-reduce.4.cloned.1.call-start = ((), (), s32[]{:S(2)}) async-start(), calls=%async_computation.3 | async-start | bytes 1048576 | tf_op jit(solution)/shard_map/psum | solution.py:74
  67.1 3.6 copy-start.5
  72.0 63.1 %collective-permute-start = (bf16[128,256,8]{1,0,2:T(8,128)(2,1)}, bf16[128,256,8]{1,0,2:T(8,128)(2,1)S(1)}, u32[]{:S(2)}, u32[]{:S(2)}) collective-permute-start(bf16[128,256,8]{1,0,2:T(8,128)(2,1)} %fusion.1), channel_id=1, source_target_pairs={{0,32},{32,64},{64,96},{96,128},{128,160},{160,192},{192,224},{224... | collective-permute-start | bytes 1572872 | tf_op jit(solution)/shard_map/ppermute | solution.py:16
  137.7 2.8 copy-start.2
  140.5 3.1 copy-start.7
  143.6 148.1 %reduce-scatter.2.cloned.1.call-start = ((), (), s32[]{:S(2)}) async-start(), calls=%async_computation.2 | async-start | bytes 2228224 | tf_op jit(solution)/shard_map/reduce_scatter | solution.py:78
  228.6 3.3 copy-start.4
  231.8 59.9 %copy-start.1 = (f32[128,512]{1,0:T(8,128)S(1)}, f32[128,512]{1,0:T(8,128)}, u32[]{:S(2)}) copy-start(f32[128,512]{1,0:T(8,128)} %param.11) | copy-start | bytes 786436
  231.8 311.5 %copy-start.6 = (f32[128,512]{1,0:T(8,128)S(1)}, f32[128,512]{1,0:T(8,128)}, u32[]{:S(2)}) copy-start(f32[128,512]{1,0:T(8,128)} %param.13) | copy-start | bytes 786436
  545.1 38.4 %copy-start.3 = (f32[128,512]{1,0:T(8,128)}, f32[128,512]{1,0:T(8,128)S(1)}, u32[]{:S(2)}) copy-start(f32[128,512]{1,0:T(8,128)S(1)} %get-tuple-element.9) | copy-start | bytes 786436
Sparse Core Ops, SparseCore 0:
  10.7 46.4 all-gather.1
  143.7 84.8 all-reduce.3
  232.0 59.6 reduce-scatter.1
